TPU v7x, 128 devices: a whole 4x4x4 slice. The times are simulated.
128 devices in a mesh: row: 4 (over x), col: 8 (over z, core), depth: 4 (over y).
Axes of the slice: x: 4, y: 4, z: 4, core: 2. Of those that a mesh axis runs over, the one named last changes fastest.
Arguments:
- policy_states: bfloat16 [1024, 5120], P(('col', 'depth'), 'row'), may hold values from -40 to 40
- reference_states: bfloat16 [1024, 5120], P(('row', 'col', 'depth')), may hold values from -40 to 40
- policy_weight: bfloat16 [5120, 81920], P('row', ('col', 'depth'))
- reference_weight: bfloat16 [5120, 81920], P(None, ('row', 'col', 'depth'))
- targets: int32 [1024], replicated, may hold values from 0 to 81919
- response_mask: int32 [1024], replicated, may hold values from 0 to 1, as said below
- pair_index: int32 [8], replicated, may hold values from 0 to 3, as said below
- chosen_flag: int32 [8], replicated, may hold values from 0 to 1, as said below
Outputs:
- loss: float32 [], replicated
- grad_states: float32 [1024, 5120], P(('col', 'depth'), 'row')
- grad_weight: float32 [5120, 81920], P('row', ('col', 'depth'))
Inputs may be any that keep to these rules, and one draw needn't show every extreme that they name: `response_mask`: in each sequence of 128 tokens the ones form one run of at least 32 tokens that begins at or after position 16. `pair_index`: each pair names exactly two sequences. `chosen_flag`: the two sequences of a pair have flags 1 and 0.
All inputs are finite; a program needn't handle non-finite values.
Results may differ from a plain program's by a relative error of at most 0.0022.
Values may be sent and summed in bfloat16 or wider, within the bound.
A program may use at most 128 MiB of HBM per device.

v0:
```python
import jax
import jax.numpy as jnp
from jax import lax
from jax.sharding import PartitionSpec as P

PAIRS = 4
LEN = 128
SEQS = 8


beta_value = 0.1
loss_scale = 256.0


def preference(ratio, pair_index, chosen_flag):
    sign = (2 * chosen_flag - 1).astype(jnp.float32)
    member = pair_index[:, None] == jnp.arange(PAIRS, dtype=jnp.int32)[None, :]
    margin = jnp.sum(jnp.where(member, (sign * ratio)[:, None], 0.0), axis=0)
    loss = -jnp.mean(jax.nn.log_sigmoid(beta_value * margin))
    slope = -loss_scale * beta_value / PAIRS * jax.nn.sigmoid(-beta_value * margin)
    weights = sign * jnp.sum(jnp.where(member, slope[None, :], 0.0), axis=1)
    return (loss, weights)


def softmax_parts(logits, peak, hits, along):
    spread = jnp.sum(jnp.exp(logits - jnp.expand_dims(peak, along)), axis=along)
    picked = jnp.sum(jnp.where(hits, logits, 0.0), axis=along)
    return (spread, picked)


def on_device(
    policy_states,
    reference_states,
    policy_weight,
    reference_weight,
    targets,
    response_mask,
    pair_index,
    chosen_flag,
):
    gathered = lax.all_gather(policy_states, ("col", "depth"), axis=0, tiled=True)
    tokens = gathered.shape[0]
    width = policy_weight.shape[1]
    groups = lax.axis_size("row")
    policy_first = lax.axis_index(("col", "depth")) * width
    reference_width = reference_weight.shape[1]
    reference_entries = lax.axis_index(("row", "col", "depth")) * reference_width + jnp.arange(
        reference_width, dtype=jnp.int32
    )
    reference_logits = jnp.dot(
        lax.all_gather(reference_states, ("row", "col", "depth"), axis=0, tiled=True),
        reference_weight,
        preferred_element_type=jnp.float32,
    )
    reference_hits = reference_entries[None, :] == targets[:, None]
    reference_local_peak = jnp.max(reference_logits, axis=1)
    mask_all = response_mask.astype(jnp.float32)
    share = tokens // groups
    block = gathered
    logits = lax.psum_scatter(
        jnp.dot(block, policy_weight, preferred_element_type=jnp.float32),
        "row",
        scatter_dimension=0,
        tiled=True,
    )
    first_row = lax.axis_index("row") * share
    local_targets = lax.dynamic_slice_in_dim(targets, first_row, share, 0)
    local_mask = lax.dynamic_slice_in_dim(mask_all, first_row, share, 0)
    hits = (policy_first + jnp.arange(width, dtype=jnp.int32))[None, :] == local_targets[:, None]
    peak = lax.pmax(jnp.max(logits, axis=1), ("col", "depth"))
    local_spread, local_picked = softmax_parts(logits, peak, hits, 1)
    spread, picked = lax.psum((local_spread, local_picked), ("col", "depth"))
    normalizer = peak + jnp.log(spread)
    policy_logp = picked - normalizer
    reference_peak = lax.pmax(reference_local_peak, ("row", "col", "depth"))
    other_spread, other_picked = softmax_parts(reference_logits, reference_peak, reference_hits, 1)
    other_spread, other_picked = lax.psum((other_spread, other_picked), ("row", "col", "depth"))
    reference_logp = other_picked - (reference_peak + jnp.log(other_spread))
    positions = first_row + jnp.arange(share, dtype=jnp.int32)
    owner = (positions // LEN)[:, None] == jnp.arange(SEQS, dtype=jnp.int32)[None, :]
    local_sums = jnp.sum(jnp.where(owner, (policy_logp * local_mask)[:, None], 0.0), axis=0)
    policy_sums = lax.psum(local_sums, "row")
    reference_sums = jnp.sum((reference_logp * mask_all).reshape(SEQS, LEN), axis=1)
    loss, weights = preference(policy_sums - reference_sums, pair_index, chosen_flag)
    token_weight = jnp.sum(jnp.where(owner, weights[None, :], 0.0), axis=1) * local_mask
    softmax_rows = jnp.exp(logits - normalizer[:, None])
    grad_logits = (token_weight[:, None] * (hits.astype(jnp.float32) - softmax_rows)).astype(
        jnp.bfloat16
    )
    piece = lax.all_gather(grad_logits, "row", axis=0, tiled=True)
    block = gathered
    weight_sum = lax.dot_general(
        block, piece, (((0,), (0,)), ((), ())), preferred_element_type=jnp.float32
    )
    rows_part = lax.dot_general(
        piece, policy_weight, (((1,), (1,)), ((), ())), preferred_element_type=jnp.float32
    )
    grad_states = lax.psum_scatter(rows_part, ("col", "depth"), scatter_dimension=0, tiled=True)
    return (loss, grad_states, weight_sum)


def solution(mesh):
    in_specs = (
        P(("col", "depth"), "row"),
        P(("row", "col", "depth"), None),
        P("row", ("col", "depth")),
        P(None, ("row", "col", "depth")),
        P(),
        P(),
        P(),
        P(),
    )
    out_specs = (P(), P(("col", "depth"), "row"), P("row", ("col", "depth")))
    return jax.shard_map(
        on_device, mesh=mesh, in_specs=in_specs, out_specs=out_specs, check_vma=False
    )
```

profile of v0, /device:TPU:0, one launch (start us, length us, event | category | flops | bytes accessed | tf_op | source)
XLA Modules:
  0.0 577.1 jit_solution(2275391657799586825)
XLA Ops:
  7.2 0.0 all-gather.4.cloned.1.call-start
  7.2 0.7 all-gather.4.cloned.1.call-update
  7.9 0.0 all-gather.6.cloned.1.call-start
  7.9 0.7 all-gather.6.cloned.1.call-update
  8.6 0.0 reduce-scatter.3.cloned.1.call-start
  8.7 48.7 %all-gather.4.cloned.1.call-done = bf16[1024,1280]{1,0:T(8,128)(2,1)} async-done(((bf16[32,1280]{1,0:T(8,128)(2,1)}), bf16[1024,1280]{1,0:T(8,128)(2,1)}) %all-gather.4.cloned.1.call-update) | async-done | bytes 2621456 | tf_op jit(solution)/shard_map/all_gather | solution.py:41
  57.4 12.7 %fusion.6 = f32[1024,2560]{1,0:T(8,128)} fusion(bf16[1024,1280]{1,0:T(8,128)(2,1)} %all-gather.4.cloned.1.call-done, bf16[1280,2560]{1,0:T(8,128)(2,1)} %param.10), kind=kOutput, calls=%fused_computation.33 | convolution fusion | flops 6710886400 | bytes 19660800 | tf_op jit(solution)/shard_map/dot_general | solution.py:61
  70.1 0.0 copy-start.1
  70.1 0.0 copy-start.2
  70.1 0.0 reduce-scatter.3.cloned.1.call-update
  70.1 0.0 all-gather.8.cloned.1.call-start
  70.2 0.6 copy-done.1
  70.8 0.0 copy-done.2
  70.8 0.1 dynamic_slice.6
  70.9 60.5 %all-gather.6.cloned.1.call-done = bf16[1024,5120]{1,0:T(8,128)(2,1)} async-done(((bf16[8,5120]{1,0:T(8,128)(2,1)}), bf16[1024,5120]{1,0:T(8,128)(2,1)}) %all-gather.6.cloned.1.call-update) | async-done | bytes 10485776 | tf_op jit(solution)/shard_map/all_gather | solution.py:51
  131.4 11.7 %fusion.5 = (f32[1024]{0:T(1024)S(1)}, f32[1024,640]{0,1:T(8,128)S(1)}) fusion(bf16[1024,5120]{1,0:T(8,128)(2,1)} %all-gather.6.cloned.1.call-done, bf16[5120,640]{1,0:T(8,128)(2,1)} %param.11), kind=kOutput, calls=%fused_computation.32 | convolution fusion | flops 6711540736 | bytes 19664896 | tf_op jit(solution)/shard_map/dot_general | solution.py:50
  143.1 67.8 %pmax.15 = f32[1024]{0:T(1024)S(1)} all-reduce(f32[1024]{0:T(1024)S(1)} %get-tuple-element.21), channel_id=1, replica_groups=mesh['row'=4,'col'=8,'depth'=4] {'row','col','depth'}, use_global_device_ids=true, to_apply=%region_12.13 | all-reduce | flops 1024 | bytes 8192 | tf_op jit(solution)/shard_map/pmax | solution.py:75
  210.9 0.6 exponential_reduce_fusion
  211.5 65.0 %all-reduce = (f32[1024]{0:T(1024)S(1)}, f32[1024]{0:T(1024)S(1)}) all-reduce(f32[1024]{0:T(1024)S(1)} %get-tuple-element.10, f32[1024]{0:T(1024)S(1)} %get-tuple-element.9), channel_id=1, replica_groups=mesh['row'=4,'col'=8,'depth'=4] {'row','col','depth'}, use_global_device_ids=true, to_apply=%region_10.11 | all-reduce | flops 2048 | bytes 16384 | tf_op jit(solution)/shard_map/psum | solution.py:77
  276.5 0.0 copy-start.3
  276.5 0.0 reduce-scatter.3.cloned.1.call-done
  276.6 0.0 copy-start
  276.6 2.1 reduce_max.18
  278.7 64.5 %pmax.14 = f32[256]{0:T(256)S(1)} all-reduce(f32[256]{0:T(256)S(1)} %reduce_max.18), channel_id=1, replica_groups=mesh['row'=4,'col'=8,'depth'=4] {'col','depth'}, use_global_device_ids=true, to_apply=%region_4.0 | all-reduce | flops 256 | bytes 2048 | tf_op jit(solution)/shard_map/pmax | solution.py:70
  343.1 0.0 copy-done
  343.1 0.7 exponential_reduce_fusion.1
  343.9 63.2 %all-reduce.1 = (f32[256]{0:T(256)S(1)}, f32[256]{0:T(256)S(1)}) all-reduce(f32[256]{0:T(256)S(1)} %get-tuple-element.12, f32[256]{0:T(256)S(1)} %get-tuple-element.11), channel_id=1, replica_groups=mesh['row'=4,'col'=8,'depth'=4] {'col','depth'}, use_global_device_ids=true, to_apply=%region_2.0 | all-reduce | flops 512 | bytes 4096 | tf_op jit(solution)/shard_map/psum | solution.py:72
  407.0 0.1 subtract_multiply_fusion
  407.1 0.1 select_reduce_fusion.2
  407.2 0.1 bitcast_reduce_fusion
  407.4 8.6 %psum.37 = f32[8]{0:T(128)S(1)} all-reduce(f32[8]{0:T(128)S(1)} %select_reduce_fusion.2), channel_id=1, replica_groups=mesh['row'=4,'col'=8,'depth'=4] {'row'}, use_global_device_ids=true, to_apply=%region_8.9 | all-reduce | flops 8 | bytes 64 | tf_op jit(solution)/shard_map/psum | solution.py:82
  416.0 0.0 copy-done.3
  416.0 0.0 copy-done.5
  416.0 0.1 select_reduce_fusion.4
  416.1 0.6 divide_multiply_fusion
  416.7 0.1 select_reduce_fusion.3
  416.8 0.1 select_reduce_fusion.1
  416.9 0.1 dynamic-slice_multiply_fusion
  417.0 1.9 fusion.3
  418.9 0.0 all-gather.8.cloned.1.call-update
  418.9 0.2 reduce-scatter.5.cloned.1.call-start
  419.1 52.5 %all-gather.8.cloned.1.call-done = bf16[1024,2560]{1,0:T(8,128)(2,1)} async-done(((bf16[256,2560]{1,0:T(8,128)(2,1)}), bf16[1024,2560]{1,0:T(8,128)(2,1)}) %all-gather.8.cloned.1.call-update) | async-done | bytes 5242896 | tf_op jit(solution)/shard_map/all_gather | solution.py:90
  471.6 12.3 %fusion.7 = f32[1024,1280]{1,0:T(8,128)} fusion(bf16[1024,2560]{1,0:T(8,128)(2,1)} %all-gather.8.cloned.1.call-done, bf16[1280,2560]{1,0:T(8,128)(2,1)} %param.10), kind=kOutput, calls=%fused_computation.34 | convolution fusion | flops 6710886400 | bytes 17039360 | tf_op jit(solution)/shard_map/dot_general | solution.py:95
  483.9 0.0 reduce-scatter.5.cloned.1.call-update
  484.8 0.9 copy-done.4
  485.7 11.7 %convolution_bitcast_fusion = f32[1280,2560]{0,1:T(8,128)} fusion(bf16[1024,2560]{1,0:T(8,128)(2,1)} %all-gather.8.cloned.1.call-done, bf16[1024,1280]{1,0:T(8,128)(2,1)S(1)} %copy-done.4), kind=kOutput, calls=%fused_computation | convolution fusion | flops 6710886400 | bytes 20971520 | tf_op jit(solution)/shard_map/dot_general | solution.py:92
  497.4 14.2 %copy.12 = f32[1280,2560]{1,0:T(8,128)} copy(f32[1280,2560]{0,1:T(8,128)} %convolution_bitcast_fusion) | data formatting | bytes 26214400
  511.6 57.8 %reduce-scatter.5.cloned.1.call-done = f32[32,1280]{1,0:T(8,128)} async-done(((f32[1024,1280]{1,0:T(8,128)}), f32[32,1280]{1,0:T(8,128)}) %reduce-scatter.5.cloned.1.call-update) | async-done | bytes 163856 | tf_op jit(solution)/shard_map/reduce_scatter | solution.py:98
  (8 shorter events, 0.0 us)
Async XLA Ops:
  7.2 50.2 %all-gather.4.cloned.1.call-start = ((), (), s32[]{:S(2)}) async-start(), calls=%async_computation.2 | async-start | bytes 2703360 | tf_op jit(solution)/shard_map/all_gather | solution.py:41
  7.9 123.5 %all-gather.6.cloned.1.call-start = ((), (), s32[]{:S(2)}) async-start(), calls=%async_computation.4 | async-start | bytes 10567680 | tf_op jit(solution)/shard_map/all_gather | solution.py:51
  8.6 267.9 %reduce-scatter.3.cloned.1.call-start = ((), (), s32[]{:S(2)}) async-start(), calls=%async_computation.3 | async-start | bytes 13107200 | tf_op jit(solution)/shard_map/reduce_scatter | solution.py:60
  70.1 0.7 copy-start.1
  70.1 0.7 copy-start.2
  70.1 401.5 %all-gather.8.cloned.1.call-start = ((), (), s32[]{:S(2)}) async-start(), calls=%async_computation.5 | async-start | bytes 6553600 | tf_op jit(solution)/shard_map/all_gather | solution.py:90
  276.5 139.5 %copy-start.3 = (s32[8]{0:T(128)S(1)}, s32[8]{0:T(128)}, u32[]{:S(2)}) copy-start(s32[8]{0:T(128)} %param.15) | copy-start | bytes 100
  276.5 139.5 %copy-start.5 = (s32[8]{0:T(128)S(1)}, s32[8]{0:T(128)}, u32[]{:S(2)}) copy-start(s32[8]{0:T(128)} %param.14) | copy-start | bytes 100
  276.6 66.6 %copy-start = (f32[256,2560]{1,0:T(8,128)S(1)}, f32[256,2560]{1,0:T(8,128)}, u32[]{:S(2)}) copy-start(f32[256,2560]{1,0:T(8,128)} %reduce-scatter.3.cloned.1.call-done) | copy-start | bytes 7864324
  418.9 150.5 %reduce-scatter.5.cloned.1.call-start = ((), (), s32[]{:S(2)}) async-start(), calls=%async_computation.6 | async-start | bytes 5406720 | tf_op jit(solution)/shard_map/reduce_scatter | solution.py:98
  483.9 1.8 copy-start.4
Sparse Core Ops, SparseCore 0:
  10.2 47.0 all-gather.3
  60.5 70.8 all-gather.5
  134.4 98.3 reduce-scatter.2
  419.0 52.5 all-gather.7
  484.1 85.2 reduce-scatter.4
where the time goes:
time: 578 us; the launch traced here: 577 us
  blocking collectives  269 us (47%)
  waiting for transfers between devices  221 us (38%)
  matrix products  48.4 us (8%)
  local copies, waits for them, and re-layouts  15.8 us (3%)
  between operations  15.8 us (3%)
  other arithmetic  6.69 us (1%)
    pmax x1, blocking collectives, on_device(): reference_peak = lax.pmax(reference_local_peak, ('row', 'col', 'depth'))  67.8 us
    psum x1, blocking collectives, on_device(): lax.psum((other_spread, other_picked), ('row', 'col', 'depth'))  65 us
    pmax x1, blocking collectives, on_device(): peak = lax.pmax(jnp.max(logits, axis=1), ('col', 'depth'))  64.5 us
    psum x1, blocking collectives, on_device(): spread, picked = lax.psum((local_spread, local_picked), ('col', 'depth'))  63.2 us
    all_gather x1, waiting for transfers between devices, on_device(): lax.all_gather(reference_states, ('row', 'col', 'depth'), axis=0, tiled=T...  60.5 us
    reduce_scatter x1, waiting for transfers between devices, on_device(): lax.psum_scatter(rows_part, ('col', 'depth'), scatter_dimension=0, tiled=...  57.8 us
    all_gather x1, waiting for transfers between devices, on_device(): piece = lax.all_gather(grad_logits, 'row', axis=0, tiled=True)  52.5 us
    all_gather x1, waiting for transfers between devices, on_device(): lax.all_gather(policy_states, ('col', 'depth'), axis=0, tiled=True)  48.7 us
  transfers between devices with their start and end apart: 5, of which 4 were waited for; matrix products, arithmetic and copies ran while one was open for 9% of the time, Pallas kernels for 0%

commit v1 on v0

v1 whole, which is shorter than its diff:
```python
import functools

import jax
import jax.numpy as jnp
from jax import lax
from jax.experimental import pallas as pl
from jax.experimental.pallas import tpu as pltpu
from jax.sharding import PartitionSpec as P

PAIRS = 4
LEN = 128
SEQS = 8
SKIP = 16
KEEP = LEN - SKIP

beta_value = 0.1
loss_scale = 256.0

MESH = pl.DeviceIdType.MESH
VMEM_LIMIT = 56 * 1024 * 1024
ROWS = 16


def preference(ratio, pair_index, chosen_flag):
    sign = (2 * chosen_flag - 1).astype(jnp.float32)
    member = pair_index[:, None] == jnp.arange(PAIRS, dtype=jnp.int32)[None, :]
    margin = jnp.sum(jnp.where(member, (sign * ratio)[:, None], 0.0), axis=0)
    loss = -jnp.mean(jax.nn.log_sigmoid(beta_value * margin))
    slope = -loss_scale * beta_value / PAIRS * jax.nn.sigmoid(-beta_value * margin)
    weights = sign * jnp.sum(jnp.where(member, slope[None, :], 0.0), axis=1)
    return (loss, weights)


class Place:
    def __init__(self):
        self.x = lax.axis_index("row")
        col = lax.axis_index("col")
        self.z = col // 2
        self.c = col % 2
        self.y = lax.axis_index("depth")

    def on_x(self, step):
        return ((self.x + step) % 4, self.z * 2 + self.c, self.y)

    def on_y(self, step):
        return (self.x, self.z * 2 + self.c, (self.y + step) % 4)

    def on_z(self, step):
        return (self.x, ((self.z + step) % 4) * 2 + self.c, self.y)

    def other_core(self):
        return (self.x, self.z * 2 + 1 - self.c, self.y)


def greet(peers):
    barrier = pltpu.get_barrier_semaphore()
    for peer in peers:
        pl.semaphore_signal(barrier, inc=1, device_id=peer, device_id_type=MESH)
    pl.semaphore_wait(barrier, len(peers))


class Mover:
    def __init__(self, send, recv):
        self.send, self.recv, self.used, self.all = send, recv, 0, []

    def start(self, src, dst, peer):
        k = self.used
        self.used += 1
        copy = pltpu.make_async_remote_copy(
            src_ref=src,
            dst_ref=dst,
            send_sem=self.send.at[k],
            recv_sem=self.recv.at[k],
            device_id=peer,
            device_id_type=MESH,
        )
        copy.start()
        self.all.append(copy)
        return copy

    def finish(self):
        for copy in self.all:
            copy.wait_send()


class Ring:
    def __init__(self, mover, me, view, peer):
        self.mover, self.me, self.view, self.peer = mover, me, view, peer

    def begin(self):
        own = self.view(self.me, None)
        self.right = self.mover.start(own, own, self.peer(1))
        self.left = self.mover.start(own, own, self.peer(3))

    def forward(self):
        self.right.wait_recv()
        part = self.view((self.me + 3) % 4, 0)
        self.far_right = self.mover.start(part, part, self.peer(1))
        self.left.wait_recv()
        part = self.view((self.me + 1) % 4, 1)
        self.far_left = self.mover.start(part, part, self.peer(3))

    def end(self):
        self.far_right.wait_recv()
        self.far_left.wait_recv()


def gather_kernel(own_ref, out, send, recv):
    at = Place()
    z, c, y = at.z, at.c, at.y
    greet([at.on_y(1), at.on_y(3), at.on_z(1), at.on_z(3), at.other_core()])
    move = Mover(send, recv)
    width = own_ref.shape[1] // 2
    low, high = pl.ds(0, width), pl.ds(width, width)
    out[z, c, y] = own_ref[...]

    def halves(half, count):
        return slice(None) if half is None else pl.ds(half * (count // 2), count // 2)

    rows = own_ref.shape[0]
    first_y = Ring(move, y, lambda i, h: out.at[z, c, i, halves(h, rows), low], at.on_y)
    first_z = Ring(move, z, lambda i, h: out.at[i, c, y, halves(h, rows), high], at.on_z)
    then_z = Ring(move, z, lambda i, h: out.at[i, c, halves(h, 4), :, low], at.on_z)
    then_y = Ring(move, y, lambda i, h: out.at[halves(h, 4), c, i, :, high], at.on_y)
    first_y.begin()
    first_z.begin()
    first_y.forward()
    first_z.forward()
    first_y.end()
    then_z.begin()
    first_z.end()
    then_y.begin()
    then_z.forward()
    then_y.forward()
    then_z.end()
    half = out.at[:, c, :, :, low]
    one = move.start(half, half, at.other_core())
    then_y.end()
    half = out.at[:, c, :, :, high]
    two = move.start(half, half, at.other_core())
    one.wait_recv()
    two.wait_recv()
    move.finish()


def gather_states(block):
    rows, width = block.shape
    out = pl.pallas_call(
        gather_kernel,
        name="gather_states",
        out_shape=jax.ShapeDtypeStruct((4, 2, 4, rows, width), block.dtype),
        in_specs=[pl.BlockSpec(memory_space=pltpu.VMEM)],
        out_specs=pl.BlockSpec(memory_space=pltpu.VMEM),
        scratch_shapes=[pltpu.SemaphoreType.DMA((18,)), pltpu.SemaphoreType.DMA((18,))],
        compiler_params=pltpu.CompilerParams(
            collective_id=0, has_side_effects=True, vmem_limit_bytes=VMEM_LIMIT
        ),
    )(block)
    return out.reshape(32 * rows, width)


def logits_kernel(
    states, weight, targets, out, stats, partial, qsend, qrecv, ssend, srecv, column, send, recv
):
    at = Place()
    x = at.x
    greet([at.on_x(1), at.on_x(3)])
    move = Mover(send, recv)
    share, width = partial.shape[1], partial.shape[2]
    half = width // 2
    tile = 512
    padded = column.shape[0]

    def product(owner):
        rows = pl.ds(pl.multiple_of(owner * share, 16), share)

        @pl.loop(0, width // tile)
        def _(j):
            cols = pl.ds(pl.multiple_of(j * tile, tile), tile)
            partial[owner, :, cols] = jnp.dot(
                states[rows, :], weight[:, cols], preferred_element_type=jnp.float32
            )

    def scale_column(k):
        row = jnp.broadcast_to(srecv[k, 0:1, :], (128, padded))
        return jnp.transpose(row)

    def pack(k, owner, side, peer, add=None):
        cols = pl.ds(side * half, half)
        if add is not None:
            column[...] = scale_column(add)

        @pl.loop(0, share // ROWS)
        def _(r):
            rows = pl.ds(pl.multiple_of(r * ROWS, ROWS), ROWS)
            value = partial[owner, rows, cols]
            if add is not None:
                value += qrecv[add, rows, :].astype(jnp.int32).astype(jnp.float32) * column[rows, 0:1]
            top = jnp.maximum(jnp.max(jnp.abs(value), axis=1, keepdims=True), 1e-30)
            step = top * (1.0 / 32767.0)
            code = jnp.round(value * (1.0 / step)).astype(jnp.int32)
            qsend[k, rows, :] = code.astype(jnp.int16)
            column[rows, :] = jnp.broadcast_to(step, (ROWS, 128))

        ssend[k] = jnp.transpose(column[...])[0:8]
        return (
            move.start(ssend.at[k], srecv.at[k], peer),
            move.start(qsend.at[k], qrecv.at[k], peer),
        )

    def arrived(pair):
        pair[0].wait_recv()
        pair[1].wait_recv()

    right, left = at.on_x(1), at.on_x(3)
    after, before, across = (x + 1) % 4, (x + 3) % 4, (x + 2) % 4
    column[...] = jnp.zeros_like(column)
    product(across)
    r0 = pack(0, across, 0, right)
    l0 = pack(3, across, 1, left)
    product(after)
    r1 = pack(1, after, 1, right)
    product(before)
    l1 = pack(4, before, 0, left)
    product(x)
    arrived(r0)
    r2 = pack(2, after, 0, right, add=0)
    arrived(l0)
    l2 = pack(5, before, 1, left, add=3)

    def add_in(k, side):
        cols = pl.ds(side * half, half)
        column[...] = scale_column(k)

        @pl.loop(0, share // ROWS)
        def _(r):
            rows = pl.ds(pl.multiple_of(r * ROWS, ROWS), ROWS)
            partial[x, rows, cols] += (
                qrecv[k, rows, :].astype(jnp.int32).astype(jnp.float32) * column[rows, 0:1]
            )

    arrived(r1)
    add_in(1, 1)
    arrived(l1)
    add_in(4, 0)
    arrived(r2)
    add_in(2, 0)
    arrived(l2)
    add_in(5, 1)

    first = (lax.axis_index("col") * 4 + lax.axis_index("depth")) * width

    @pl.loop(0, share // ROWS)
    def _(r):
        rows = pl.ds(pl.multiple_of(r * ROWS, ROWS), ROWS)
        logits = partial[x, rows, :]
        peak = jnp.max(logits, axis=1, keepdims=True)
        spread = jnp.exp(logits - peak)
        out[x, rows, :] = spread.astype(jnp.bfloat16)
        total = jnp.sum(spread, axis=1, keepdims=True)
        wanted = targets[pl.ds(pl.multiple_of(x * share, 16) + r * ROWS, ROWS), :]
        hits = lax.broadcasted_iota(jnp.int32, (ROWS, width), 1) + first == wanted
        picked = jnp.sum(jnp.where(hits, logits, 0.0), axis=1, keepdims=True)
        lane = lax.broadcasted_iota(jnp.int32, (ROWS, 128), 1)
        column[rows, :] = jnp.where(lane == 0, peak, jnp.where(lane == 1, total, picked))

    def part(i, side):
        return out.at[i] if side is None else out.at[i, :, pl.ds(side * half, half)]

    ring = Ring(move, x, part, at.on_x)
    ring.begin()
    stats[...] = jnp.transpose(column[...])[0:8]
    ring.forward()
    ring.end()
    move.finish()


def spread_logits(states, weight, targets):
    tokens, width = states.shape[0], weight.shape[1]
    share = tokens // 4
    padded = 256
    vmem = pl.BlockSpec(memory_space=pltpu.VMEM)
    return pl.pallas_call(
        logits_kernel,
        name="spread_logits",
        out_shape=(
            jax.ShapeDtypeStruct((4, share, width), jnp.bfloat16),
            jax.ShapeDtypeStruct((8, padded), jnp.float32),
        ),
        in_specs=[vmem] * 3,
        out_specs=(vmem, vmem),
        scratch_shapes=[
            pltpu.VMEM((4, share, width), jnp.float32),
            pltpu.VMEM((6, share, width // 2), jnp.int16),
            pltpu.VMEM((6, share, width // 2), jnp.int16),
            pltpu.VMEM((6, 8, padded), jnp.float32),
            pltpu.VMEM((6, 8, padded), jnp.float32),
            pltpu.VMEM((padded, 128), jnp.float32),
            pltpu.SemaphoreType.DMA((16,)),
            pltpu.SemaphoreType.DMA((16,)),
        ],
        compiler_params=pltpu.CompilerParams(
            collective_id=1, has_side_effects=True, vmem_limit_bytes=VMEM_LIMIT
        ),
    )(states, weight, targets)


def merge(a, b):
    peak = jnp.maximum(a[..., 0:1, :], b[..., 0:1, :])
    total = a[..., 1:2, :] * jnp.exp(a[..., 0:1, :] - peak) + b[..., 1:2, :] * jnp.exp(
        b[..., 0:1, :] - peak
    )
    return jnp.concatenate([peak, total, a[..., 2:3, :] + b[..., 2:3, :], a[..., 3:, :]], axis=-2)


def stats_kernel(policy, other, out, first, held, got, send, recv):
    at = Place()
    x = at.x
    ways = [at.on_x, at.on_y, at.on_z]
    greet([way(i) for way in ways for i in (1, 2, 3)] + [at.other_core()])
    move = Mover(send, recv)
    copies = [
        move.start(other.at[(x + i) % 4], first.at[i - 1], at.on_x(i)) for i in (1, 2, 3)
    ]
    mine = other[x]
    for i in (0, 1, 2):
        copies[i].wait_recv()
        mine = merge(mine, first[i])
    both = jnp.stack([policy[...], mine])
    stages = [[at.other_core()], [at.on_y(i) for i in (1, 2, 3)], [at.on_z(i) for i in (1, 2, 3)]]
    slot = 0
    for s, peers in enumerate(stages):
        held[s] = both
        copies = []
        for peer in peers:
            copies.append((slot, move.start(held.at[s], got.at[slot], peer)))
            slot += 1
        for k, copy in copies:
            copy.wait_recv()
            both = merge(both, got[k])
    out[x] = both
    copies = [move.start(out.at[x], out.at[x], at.on_x(i)) for i in (1, 2, 3)]
    for copy in copies:
        copy.wait_recv()
    move.finish()


def combine_stats(policy, other):
    vmem = pl.BlockSpec(memory_space=pltpu.VMEM)
    padded = policy.shape[1]
    return pl.pallas_call(
        stats_kernel,
        name="combine_stats",
        out_shape=jax.ShapeDtypeStruct((4, 2, 8, padded), jnp.float32),
        in_specs=[vmem] * 2,
        out_specs=vmem,
        scratch_shapes=[
            pltpu.VMEM((3, 8, padded), jnp.float32),
            pltpu.VMEM((3, 2, 8, padded), jnp.float32),
            pltpu.VMEM((7, 2, 8, padded), jnp.float32),
            pltpu.SemaphoreType.DMA((13,)),
            pltpu.SemaphoreType.DMA((13,)),
        ],
        compiler_params=pltpu.CompilerParams(
            collective_id=2, has_side_effects=True, vmem_limit_bytes=VMEM_LIMIT
        ),
    )(policy, other)


def rows_kernel(part, out, core, by_z, by_y, sum_z, sum_y, send, recv):
    at = Place()
    z, c, y = at.z, at.c, at.y
    ways = [at.on_y, at.on_z]
    greet([way(i) for way in ways for i in (1, 2, 3)] + [at.other_core()])
    move = Mover(send, recv)
    width = part.shape[4] // 2
    sides = (pl.ds(0, width), pl.ds(width, width))
    first = [
        move.start(part.at[:, 1 - c, :, :, side], core.at[i], at.other_core())
        for i, side in enumerate(sides)
    ]
    first[0].wait_recv()
    first[1].wait_recv()

    @pl.loop(0, 16)
    def _(k):
        core[0, k // 4, k % 4] += part[k // 4, c, k % 4, :, sides[0]]
        core[1, k // 4, k % 4] += part[k // 4, c, k % 4, :, sides[1]]

    a = [move.start(core.at[0, (z + i) % 4], by_z.at[i - 1], at.on_z(i)) for i in (1, 3, 2)]
    b = [move.start(core.at[1, :, (y + i) % 4], by_y.at[i - 1], at.on_y(i)) for i in (1, 3, 2)]
    for copy in a:
        copy.wait_recv()

    @pl.loop(0, 4)
    def _(k):
        sum_z[k] = core[0, z, k] + by_z[0, k] + by_z[1, k] + by_z[2, k]

    a = [
        move.start(sum_z.at[(y + i) % 4], by_z.at[3, i - 1], at.on_y(i)) for i in (1, 3, 2)
    ]
    for copy in b:
        copy.wait_recv()

    @pl.loop(0, 4)
    def _(k):
        sum_y[k] = core[1, k, y] + by_y[0, k] + by_y[1, k] + by_y[2, k]

    b = [
        move.start(sum_y.at[(z + i) % 4], by_y.at[3, i - 1], at.on_z(i)) for i in (1, 3, 2)
    ]
    for copy in a:
        copy.wait_recv()
    out[:, sides[0]] = sum_z[y] + by_z[3, 0] + by_z[3, 1] + by_z[3, 2]
    for copy in b:
        copy.wait_recv()
    out[:, sides[1]] = sum_y[z] + by_y[3, 0] + by_y[3, 1] + by_y[3, 2]
    move.finish()


def scatter_rows(part):
    vmem = pl.BlockSpec(memory_space=pltpu.VMEM)
    rows, width = part.shape[0] // 32, part.shape[1]
    half = width // 2
    return pl.pallas_call(
        rows_kernel,
        name="scatter_rows",
        out_shape=jax.ShapeDtypeStruct((rows, width), jnp.float32),
        in_specs=[vmem],
        out_specs=vmem,
        scratch_shapes=[
            pltpu.VMEM((2, 4, 4, rows, half), jnp.float32),
            pltpu.VMEM((4, 4, rows, half), jnp.float32),
            pltpu.VMEM((4, 4, rows, half), jnp.float32),
            pltpu.VMEM((4, rows, half), jnp.float32),
            pltpu.VMEM((4, rows, half), jnp.float32),
            pltpu.SemaphoreType.DMA((14,)),
            pltpu.SemaphoreType.DMA((14,)),
        ],
        compiler_params=pltpu.CompilerParams(
            collective_id=3, has_side_effects=True, vmem_limit_bytes=VMEM_LIMIT
        ),
    )(part.reshape(4, 2, 4, rows, width))


def on_device(
    policy_states,
    reference_states,
    policy_weight,
    reference_weight,
    targets,
    response_mask,
    pair_index,
    chosen_flag,
):
    width = policy_weight.shape[1]
    reference_width = reference_weight.shape[1]
    mask_all = response_mask.astype(jnp.float32)
    others = lax.all_gather(reference_states, ("row", "col", "depth"), axis=0, tiled=True)

    gathered = gather_states(policy_states)
    tokens = SEQS * KEEP
    states = gathered.reshape(SEQS, LEN, -1)[:, SKIP:].reshape(tokens, -1)
    kept_targets = targets.reshape(SEQS, LEN)[:, SKIP:].reshape(tokens, 1)
    kept_mask = mask_all.reshape(SEQS, LEN)[:, SKIP:].reshape(tokens)
    sequence = jnp.arange(tokens, dtype=jnp.int32) // KEEP
    spread, policy_stats = spread_logits(states, policy_weight, kept_targets)

    reference_entries = lax.axis_index(("row", "col", "depth")) * reference_width + jnp.arange(
        reference_width, dtype=jnp.int32
    )
    others, spread = lax.optimization_barrier((others, spread))
    reference_logits = jnp.dot(others, reference_weight, preferred_element_type=jnp.float32)
    reference_peak = jnp.max(reference_logits, axis=1)
    reference_total = jnp.sum(jnp.exp(reference_logits - reference_peak[:, None]), axis=1)
    hits = reference_entries[None, :] == targets[:, None]
    reference_picked = jnp.sum(jnp.where(hits, reference_logits, 0.0), axis=1)
    reference_stats = jnp.zeros((4, 8, 256), jnp.float32)
    reference_stats = reference_stats.at[:, 0].set(reference_peak.reshape(4, 256))
    reference_stats = reference_stats.at[:, 1].set(reference_total.reshape(4, 256))
    reference_stats = reference_stats.at[:, 2].set(reference_picked.reshape(4, 256))

    local_peak = policy_stats[0:1]
    policy_stats = jnp.concatenate([policy_stats[:3], local_peak, policy_stats[4:]], axis=0)
    merged = combine_stats(policy_stats, reference_stats)
    share = tokens // 4
    mine = merged[:, 0, :, :share]
    normalizer = (mine[:, 0] + jnp.log(mine[:, 1])).reshape(tokens)
    policy_logp = mine[:, 2].reshape(tokens) - normalizer
    peak = mine[:, 3].reshape(tokens)
    theirs = merged[:, 1]
    reference_logp = (theirs[:, 2] - theirs[:, 0] - jnp.log(theirs[:, 1])).reshape(SEQS, LEN)
    member = sequence[:, None] == jnp.arange(SEQS, dtype=jnp.int32)[None, :]
    policy_sums = jnp.sum(jnp.where(member, (policy_logp * kept_mask)[:, None], 0.0), axis=0)
    reference_sums = jnp.sum(reference_logp * mask_all.reshape(SEQS, LEN), axis=1)
    loss, weights = preference(policy_sums - reference_sums, pair_index, chosen_flag)
    token_weight = jnp.sum(jnp.where(member, weights[None, :], 0.0), axis=1) * kept_mask

    entries = lax.axis_index(("col", "depth")) * width + jnp.arange(width, dtype=jnp.int32)
    hits = entries[None, :] == kept_targets
    softmax = spread.reshape(tokens, width).astype(jnp.float32) * jnp.exp(peak - normalizer)[:, None]
    grad_logits = (token_weight[:, None] * (hits.astype(jnp.float32) - softmax)).astype(jnp.bfloat16)
    rows_part = lax.dot_general(
        grad_logits, policy_weight, (((1,), (1,)), ((), ())), preferred_element_type=jnp.float32
    )
    rows_part = jnp.pad(rows_part.reshape(SEQS, KEEP, -1), ((0, 0), (SKIP, 0), (0, 0)))
    grad_states = scatter_rows(rows_part.reshape(SEQS * LEN, -1))
    grad_weight = lax.dot_general(
        states, grad_logits, (((0,), (0,)), ((), ())), preferred_element_type=jnp.float32
    )
    return (loss, grad_states, grad_weight)


def solution(mesh):
    in_specs = (
        P(("col", "depth"), "row"),
        P(("row", "col", "depth"), None),
        P("row", ("col", "depth")),
        P(None, ("row", "col", "depth")),
        P(),
        P(),
        P(),
        P(),
    )
    out_specs = (P(), P(("col", "depth"), "row"), P("row", ("col", "depth")))
    return jax.shard_map(
        on_device, mesh=mesh, in_specs=in_specs, out_specs=out_specs, check_vma=False
    )
```

time: 578 us -> 276 us (0.48)
  blocking collectives: 269 us -> 0 us
  waiting for transfers between devices: 221 us -> 0.68 us
  Pallas kernels: 0 us -> 191 us
  matrix products: 48.4 us -> 32.6 us
  local copies, waits for them, and re-layouts: 15.8 us -> 27.5 us
    pallas_call x0 -> x4, Pallas kernels: none -> 191 us  [the longest x1 113 us: spread_logits(): pl.pallas_call(logits_kernel, name='spread_logits', out_shape=(jax.ShapeD...]
    psum x3 -> x0, blocking collectives: 137 us -> none  [the longest x1 65 us: on_device(): lax.psum((other_spread, other_picked), ('row', 'col', 'depth'))]
    pmax x2 -> x0, blocking collectives: 132 us -> none  [the longest x1 67.8 us: on_device(): reference_peak = lax.pmax(reference_local_peak, ('row', 'col', 'depth'))]
    all_gather x2 -> x0, waiting for transfers between devices: 101 us -> none  [the longest x1 52.5 us: on_device(): piece = lax.all_gather(grad_logits, 'row', axis=0, tiled=True)]
    all_gather x1, waiting for transfers between devices: 60.5 us -> 0.01 us  [on_device(): lax.all_gather(reference_states, ('row', 'col', 'depth'), axis=0, tiled=T...]
    reduce_scatter x2 -> x0, waiting for transfers between devices: 57.8 us -> none  [the longest x1 57.8 us: on_device(): lax.psum_scatter(rows_part, ('col', 'depth'), scatter_dimension=0, tiled=...]
    dot_general x4 -> x3, matrix products: 48.4 us -> 32.6 us  [the longest x1 11.7 us: on_device(): jnp.dot(others, reference_weight, preferred_element_type=jnp.float32)]
    slice x0 -> x6, local copies, waits for them, and re-layouts: none -> 6.12 us  [the longest x1 3.19 us: on_device(): states = gathered.reshape(SEQS, LEN, -1)[:, SKIP:].reshape(tokens, -1)]
  transfers between devices with their start and end apart: 5 -> 1, of which waited for: 4 -> 0; matrix products, arithmetic and copies ran while one was open for 9% -> 3% of each run, Pallas kernels for 0% -> 51%
where the time goes in v1:
time: 276 us; the launch traced here: 274 us
  Pallas kernels  191 us (69%)
  matrix products  32.6 us (12%)
  local copies, waits for them, and re-layouts  27.5 us (10%)
  between operations  16 us (6%)
  other arithmetic  5.73 us (2%)
    pallas_call x1, Pallas kernels, spread_logits(): pl.pallas_call(logits_kernel, name='spread_logits', out_shape=(jax.ShapeD...  113 us
    pallas_call x1, Pallas kernels, scatter_rows(): pl.pallas_call(rows_kernel, name='scatter_rows', out_shape=jax.ShapeDtype...  31.8 us
    pallas_call x1, Pallas kernels, gather_states(): pl.pallas_call(gather_kernel, name='gather_states', out_shape=jax.ShapeDt...  26.1 us
    pallas_call x1, Pallas kernels, combine_stats(): pl.pallas_call(stats_kernel, name='combine_stats', out_shape=jax.ShapeDty...  20 us
    unnamed x21, local copies, waits for them, and re-layouts  15.2 us
    dot_general x1, matrix products, on_device(): jnp.dot(others, reference_weight, preferred_element_type=jnp.float32)  11.7 us
    dot_general x1, matrix products, on_device(): lax.dot_general(grad_logits, policy_weight, (((1,), (1,)), ((), ())), pre...  10.8 us
    dot_general x1, matrix products, on_device(): lax.dot_general(states, grad_logits, (((0,), (0,)), ((), ())), preferred_...  10.1 us
  transfers between devices with their start and end apart: 1, of which 0 were waited for; matrix products, arithmetic and copies ran while one was open for 3% of the time, Pallas kernels for 51%

profile of v1, /device:TPU:0, one launch (start us, length us, event | category | flops | bytes accessed | tf_op | source)
XLA Modules:
  0.0 273.6 jit_solution(6166390459632587950)
XLA Ops:
  7.2 0.0 all-gather.2.cloned.1.call-start
  7.2 0.7 all-gather.2.cloned.1.call-update
  7.9 0.7 convert_bitcast_fusion
  8.6 0.1 slice.113
  8.7 0.1 reshape.276
  8.7 0.1 reshape.275
  8.8 0.8 slice.105
  9.6 0.1 eq.81
  9.7 1.0 reshape.279.targets
  10.6 26.1 %gather_states.1 = bf16[4,2,4,32,1280]{4,3,2,1,0:T(8,128)(2,1)} custom-call(bf16[32,1280]{1,0:T(8,128)(2,1)} %own_ref.1), custom_call_target="tpu_custom_call" | custom-call | tf_op jit(solution)/shard_map/gather_states/pallas_call | solution.py:148
  36.7 3.2 %slice.119 = bf16[8,112,1280]{2,1,0:T(8,128)(2,1)} slice(bf16[8,128,1280]{2,1,0:T(8,128)(2,1)} %bitcast.32), slice={[0:8], [16:128], [0:1280]} | slice | bytes 4587520 | tf_op jit(solution)/shard_map/slice | solution.py:463
  39.9 113.2 %spread_logits.1 = (bf16[4,224,2560]{2,1,0:T(8,128)(2,1)}, f32[8,256]{1,0:T(8,128)}) custom-call(bf16[896,1280]{1,0:T(8,128)(2,1)} %bitcast.33, bf16[1280,2560]{1,0:T(8,128)(2,1)} %weight.1, s32[896,1]{1,0:T(8,128)} %reshape.279.targets), custom_call_target="tpu_custom_call" | custom-call | tf_op jit(solution)/shard_map/spread_logits/pallas_call | solution.py:283
  153.1 0.7 slice.107
  153.8 0.7 slice.108
  154.5 0.7 slice.106
  155.2 0.6 pad_maximum_fusion.policy
  155.9 0.0 copy-start.5
  155.9 0.0 copy-start.6
  155.9 11.7 %fusion.16 = (f32[1024]{0:T(1024)S(1)}, f32[1024,640]{0,1:T(8,128)S(1)}) fusion(bf16[1024,5120]{1,0:T(8,128)(2,1)} %all-gather.2.cloned.1.call-done, bf16[5120,640]{1,0:T(8,128)(2,1)} %param.17), kind=kOutput, calls=%fused_computation.49 | convolution fusion | flops 6711540736 | bytes 19664896 | tf_op jit(solution)/shard_map/dot_general | solution.py:473
  167.6 0.0 copy-done.3
  167.6 0.6 select_reduce_fusion
  168.3 0.2 scatter.14.other
  168.5 0.0 copy-start.2
  168.5 0.6 copy-done.2
  169.1 20.0 %combine_stats.1 = f32[4,2,8,256]{3,2,1,0:T(8,128)} custom-call(f32[8,256]{1,0:T(8,128)} %pad_maximum_fusion.policy, f32[4,8,256]{2,1,0:T(8,128)} %copy-done.2), custom_call_target="tpu_custom_call" | custom-call | tf_op jit(solution)/shard_map/combine_stats/pallas_call | solution.py:351
  189.2 0.8 slice_bitcast_fusion
  189.9 0.8 slice_bitcast_fusion.1
  190.7 0.0 copy-done.4
  190.8 0.1 multiply_reduce_fusion
  190.9 0.1 sub.66
  191.0 0.1 select_reduce_fusion.2
  191.1 0.0 copy-done.5
  191.1 0.0 copy-done.6
  191.1 0.1 select_reduce_fusion.4
  191.2 0.6 divide_multiply_fusion
  191.9 0.1 select_reduce_fusion.3
  191.9 0.1 select_reduce_fusion.1
  192.0 0.1 reduce_sum.85
  192.1 0.1 reduce_sum.84
  192.2 0.1 exp.33
  192.9 0.1 slice_multiply_fusion
  193.0 10.8 %fusion = f32[8,112,1280]{2,1,0:T(8,128)S(1)} fusion(bf16[1280,2560]{1,0:T(8,128)(2,1)} %weight.1, f32[8,112]{1,0:T(8,128)S(1)} %exp.33, s32[8,112]{1,0:T(8,128)S(1)} %slice.105, s32[2560]{0:T(1024)S(1)} %iota_add_fusion, f32[8,112]{1,0:T(8,128)S(1)} %slice_multiply_fusion, bf16[8,112,2560]{2,1,0:T(8,128)(2,1)} %bitcast.35), kind=kOutput, calls=%fused_computation.3 | convolution fusion | flops 5888081920 | bytes 15749632 | tf_op jit(solution)/shard_map/dot_general | solution.py:503
  203.8 2.8 %pad.11 = f32[8,128,1280]{2,1,0:T(8,128)} pad(f32[8,112,1280]{2,1,0:T(8,128)S(1)} %fusion, f32[]{:T(128)} %constant.122.clone.1), padding=0_0x16_0x0_0 | pad | bytes 9830404 | tf_op jit(solution)/shard_map/jit(_pad)/pad | solution.py:506
  206.7 31.8 %scatter_rows.1 = f32[32,1280]{1,0:T(8,128)} custom-call(f32[4,2,4,32,1280]{4,3,2,1,0:T(8,128)} %bitcast.31), custom_call_target="tpu_custom_call" | custom-call | tf_op jit(solution)/shard_map/scatter_rows/pallas_call | solution.py:425
  238.5 2.5 multiply_convert_fusion
  241.0 10.1 %convolution_bitcast_fusion = f32[1280,2560]{0,1:T(8,128)} fusion(bf16[896,2560]{1,0:T(8,128)(2,1)S(1)} %bitcast.38, bf16[896,1280]{1,0:T(8,128)(2,1)S(1)} %bitcast.34), kind=kOutput, calls=%fused_computation | convolution fusion | flops 5872025600 | bytes 19988480 | tf_op jit(solution)/shard_map/dot_general | solution.py:508
  251.0 13.9 %copy.15 = f32[1280,2560]{1,0:T(8,128)} copy(f32[1280,2560]{0,1:T(8,128)} %convolution_bitcast_fusion) | data formatting | bytes 26214400
  265.0 0.7 copy.22
  (24 shorter events, 0.2 us)
Async XLA Ops:
  7.2 148.7 %all-gather.2.cloned.1.call-start = ((), (), s32[]{:S(2)}) async-start(), calls=%async_computation | async-start | bytes 10567680 | tf_op jit(solution)/shard_map/all_gather | solution.py:459
  155.9 11.7 %copy-start.3 = (s32[1024]{0:T(1024)S(1)}, s32[1024]{0:T(1024)}, u32[]{:S(2)}) copy-start(s32[1024]{0:T(1024)} %param.18) | copy-start | bytes 12292
  155.9 34.9 %copy-start.4 = (s32[1024]{0:T(1024)S(1)}, s32[1024]{0:T(1024)}, u32[]{:S(2)}) copy-start(s32[1024]{0:T(1024)} %param.19) | copy-start | bytes 12292
  155.9 35.2 %copy-start.5 = (s32[8]{0:T(128)S(1)}, s32[8]{0:T(128)}, u32[]{:S(2)}) copy-start(s32[8]{0:T(128)} %param.21) | copy-start | bytes 100
  155.9 35.2 %copy-start.6 = (s32[8]{0:T(128)S(1)}, s32[8]{0:T(128)}, u32[]{:S(2)}) copy-start(s32[8]{0:T(128)} %param.20) | copy-start | bytes 100
  168.5 0.6 copy-start.2
  193.0 45.4 %slice-start = ((s8[4587520]{0:T(1024)(128)(4,1)}), s8[4194304]{0:T(1024)(128)(4,1)S(1)}, s32[]{:S(2)}) async-start(s8[4587520]{0:T(1024)(128)(4,1)} %bitcast.36), calls=%async_computation.1 | async-start | bytes 8388608
  193.0 45.4 %slice-start.1 = ((s8[4587520]{0:T(1024)(128)(4,1)}), s8[393216]{0:T(1024)(128)(4,1)S(1)}, s32[]{:S(2)}) async-start(s8[4587520]{0:T(1024)(128)(4,1)} %bitcast.36), calls=%async_computation.2 | async-start | bytes 786432
  206.7 34.3 %copy-start = (bf16[8,112,1280]{2,1,0:T(8,128)(2,1)S(1)}, bf16[8,112,1280]{2,1,0:T(8,128)(2,1)}, u32[]{:S(2)}) copy-start(bf16[8,112,1280]{2,1,0:T(8,128)(2,1)} %slice.119) | copy-start | bytes 6881284
  251.0 13.9 %copy-start.1 = (f32[32,1280]{1,0:T(8,128)S(1)}, f32[32,1280]{1,0:T(8,128)}, u32[]{:S(2)}) copy-start(f32[32,1280]{1,0:T(8,128)} %scatter_rows.1) | copy-start | bytes 491524
Sparse Core Ops, SparseCore 0:
  11.1 87.9 all-gather.1
